TPU v7x, 256 devices: a whole 4x4x8 slice. The times are simulated.
256 devices in a mesh: rep: 4 (over z_lo), fsdp: 64 (over x, z_hi, y, core).
Axes of the slice: x: 4, y: 4, z: 8 (z_hi: 2, z_lo: 4; z = z_hi * 4 + z_lo), core: 2. Of those that a mesh axis runs over, the one named last changes fastest.
Arguments:
- acts: bfloat16 [196608, 8192], P(('rep', 'fsdp')), may hold values from -24 to 24
- cotangent: bfloat16 [196608, 512], P(('rep', 'fsdp')), may hold values from -0.02734375 to 0.02734375
- momentum: float32 [4, 8192, 512], P('rep', 'fsdp'), may hold values from -6 to 6
- params: float32 [8192, 512], P('fsdp'), may hold values from -0.6 to 0.6
- band_index: int32 [128, 8, 128], P('fsdp'), may hold values from 0 to 2015, as said below
Outputs:
- new_momentum: float32 [4, 8192, 512], P('rep', 'fsdp')
- new_params: float32 [8192, 512], P('fsdp')
Inputs may be any that keep to these rules, and one draw needn't show every extreme that they name: `band_index`: each entry is 64 * k + l with k and l below 32; the 128 entries of one block are distinct and the first is 0.
All inputs are finite; a program needn't handle non-finite values.
Results may differ from a plain program's by a relative error of at most 0.0003.
Values may be sent and summed in bfloat16 or wider, within the bound.
A program may use at most 192 MiB of HBM per device.

v0:
```python
import jax
import jax.numpy as jnp
from jax import lax
from jax.sharding import PartitionSpec as P

CH = 64


beta_decay = 0.9
step_rate = 0.1
soft_width = 0.05


def dct_basis(size):
    freq = jnp.arange(size, dtype=jnp.float32)[:, None]
    cell = jnp.arange(size, dtype=jnp.float32)[None, :]
    weight = jnp.where(freq == 0, jnp.sqrt(1.0 / size), jnp.sqrt(2.0 / size))
    return weight * jnp.cos(jnp.pi * (2.0 * cell + 1.0) * freq / (2.0 * size))


def encode(field, basis):
    height, breadth = field.shape
    blocks = field.reshape(height // CH, CH, breadth // CH, CH)
    coeffs = jnp.einsum("ki,aibj,lj->abkl", basis, blocks, basis, precision=lax.Precision.HIGHEST)
    return coeffs.reshape(height // CH, breadth // CH, CH * CH)


def decode(flat, basis):
    first_n, second_n = (flat.shape[0], flat.shape[1])
    coeffs = flat.reshape(first_n, second_n, CH, CH)
    field = jnp.einsum("ki,abkl,lj->aibj", basis, coeffs, basis, precision=lax.Precision.HIGHEST)
    return field.reshape(first_n * CH, second_n * CH)


def place_band(values, band_index):
    first_n, second_n = (values.shape[0], values.shape[1])
    empty = jnp.zeros((first_n, second_n, CH * CH), values.dtype)
    first_axis = jnp.arange(first_n, dtype=jnp.int32)[:, None, None]
    second_axis = jnp.arange(second_n, dtype=jnp.int32)[None, :, None]
    return empty.at[first_axis, second_axis, band_index].set(values)


def token_product(inputs, outputs):
    return lax.dot_general(
        inputs, outputs, (((0,), (0,)), ((), ())), preferred_element_type=jnp.float32
    )


def per_device(acts, cotangent, momentum, params, band_index):
    gradient = lax.psum_scatter(
        token_product(acts, cotangent), "fsdp", scatter_dimension=0, tiled=True
    )
    basis = dct_basis(CH)
    mixed = beta_decay * momentum[0] + gradient
    coeffs = encode(mixed, basis)
    band_values = jnp.take_along_axis(coeffs, band_index, axis=2)
    new_momentum = mixed - decode(place_band(band_values, band_index), basis)
    gathered = lax.all_gather(band_values[None], "rep", axis=0, tiled=True)
    shared = jnp.sum(gathered, axis=0) / gathered.shape[0]
    decoded = decode(place_band(shared, band_index), basis)
    update = decoded / jnp.sqrt(decoded * decoded + soft_width * soft_width)
    new_params = params - step_rate * update
    return (new_momentum[None], new_params)


def solution(mesh):
    return jax.shard_map(
        per_device,
        mesh=mesh,
        in_specs=(
            P(("rep", "fsdp"), None),
            P(("rep", "fsdp"), None),
            P("rep", "fsdp", None),
            P("fsdp", None),
            P("fsdp", None, None),
        ),
        out_specs=(P("rep", "fsdp", None), P("fsdp", None)),
        check_vma=False,
    )
```

profile of v0, /device:TPU:32, one launch (start us, length us, event | category | flops | bytes accessed | tf_op | source)
XLA Modules:
  0.0 535.5 jit_solution(5991889304412768023)
XLA Ops:
  7.2 1.1 copy-done
  8.3 14.9 %fusion.40 = f32[8192,512]{1,0:T(8,128)} fusion(bf16[768,8192]{1,0:T(8,128)(2,1)} %param.5, bf16[768,512]{1,0:T(8,128)(2,1)S(1)} %copy-done), kind=kOutput, calls=%fused_computation.59 | convolution fusion | flops 6442450944 | bytes 30146560 | tf_op jit(solution)/shard_map/dot_general | solution.py:44
  23.3 0.6 copy-done.3
  24.1 444.5 %reduce-scatter.2.cloned.1.call-done = f32[128,512]{1,0:T(8,128)} async-done(((f32[8192,512]{1,0:T(8,128)}), f32[128,512]{1,0:T(8,128)}) %reduce-scatter.2.cloned.1.call-update) | async-done | bytes 262160 | tf_op jit(solution)/shard_map/reduce_scatter | solution.py:50
  468.7 1.0 bitcast_add_fusion
  469.8 0.7 fusion
  470.6 0.7 fusion.12
  471.3 0.2 reshape.58
  471.4 16.2 %gather_fusion = f32[2048]{0:T(1024)S(1)} fusion(f32[2,8,4096]{2,1,0:T(8,128)S(1)} %reshape.58, s32[2048]{0:T(1024)S(1)} %or_bitcast_fusion), kind=kCustom, calls=%fused_computation | custom fusion | bytes 40960 | tf_op jit(solution)/shard_map/jit(take_along_axis)/gather | solution.py:56
  487.7 8.1 %scatter_custom_fusion = f32[65536]{0:T(1024)S(1)} fusion(s32[2048]{0:T(1024)S(1)} %select_bitcast_fusion, f32[2048]{0:T(1024)S(1)} %fusion.48, f32[]{:T(128)} %constant.16.clone.1), kind=kCustom, calls=%fused_computation.12 | custom fusion | bytes 262148
  495.9 0.1 reshape.59
  496.0 0.7 fusion.10
  496.8 0.7 convolution_bitcast_fusion.1
  497.5 0.3 copy.20
  497.8 0.1 reshape.60
  497.9 0.7 subtract_bitcast_fusion
  498.7 18.9 %all-gather = f32[8,8,128]{2,1,0:T(8,128)S(1)} all-gather(f32[2,8,128]{2,1,0:T(8,128)S(1)} %bitcast_select_fusion), channel_id=2, replica_groups=mesh['rep'=4,'fsdp'=64] {'rep'}, dimensions={0}, use_global_device_ids=true | all-gather | bytes 40960 | tf_op jit(solution)/shard_map/all_gather | solution.py:58
  517.6 8.1 %scatter_custom_fusion.1 = f32[65536]{0:T(1024)S(1)} fusion(s32[2048]{0:T(1024)S(1)} %select_bitcast_fusion, f32[2048]{0:T(1024)S(1)} %multiply_bitcast_fusion, f32[]{:T(128)} %constant.16.clone.1), kind=kCustom, calls=%fused_computation.10 | custom fusion | bytes 262148
  525.8 0.1 reshape.61
  525.9 0.7 fusion.7
  526.7 0.7 convolution_bitcast_fusion
  527.4 0.3 copy.23
  527.7 0.1 reshape.62
  527.8 0.8 multiply_subtract_fusion
  (25 shorter events, 0.4 us)
Async XLA Ops:
  7.2 1.1 copy-start
  7.2 461.5 %reduce-scatter.2.cloned.1.call-start = ((), (), s32[]{:S(2)}) async-start(), calls=%async_computation.1 | async-start | bytes 17039360 | tf_op jit(solution)/shard_map/reduce_scatter | solution.py:50
  23.2 0.7 copy-start.3
  23.3 0.7 copy-start.4
  23.3 0.8 copy-start.5
  23.3 445.4 %copy-start.1 = (f32[1,128,512]{2,1,0:T(8,128)S(1)}, f32[1,128,512]{2,1,0:T(8,128)}, u32[]{:S(2)}) copy-start(f32[1,128,512]{2,1,0:T(8,128)} %param.7) | copy-start | bytes 786436
  23.3 504.6 %copy-start.2 = (f32[128,512]{1,0:T(8,128)S(1)}, f32[128,512]{1,0:T(8,128)}, u32[]{:S(2)}) copy-start(f32[128,512]{1,0:T(8,128)} %param.8) | copy-start | bytes 786436
Sparse Core Ops, SparseCore 0:
  23.4 445.2 reduce-scatter.1
where the time goes:
time: 536 us; the launch traced here: 535 us
  waiting for transfers between devices  445 us (83%)
  local copies, waits for them, and re-layouts  35.8 us (7%)
  matrix products  19.2 us (4%)
  blocking collectives  18.9 us (4%)
  between operations  14.2 us (3%)
    reduce_scatter x1, waiting for transfers between devices, per_device(): lax.psum_scatter(token_product(acts, cotangent), 'fsdp', scatter_dimensio...  445 us
    all_gather x1, blocking collectives, per_device(): gathered = lax.all_gather(band_values[None], 'rep', axis=0, tiled=True)  18.9 us
    unnamed x14, local copies, waits for them, and re-layouts  18 us
    gather x1, local copies, waits for them, and re-layouts, per_device(): band_values = jnp.take_along_axis(coeffs, band_index, axis=2)  16.2 us
    dot_general x1, matrix products, token_product(): lax.dot_general(inputs, outputs, (((0,), (0,)), ((), ())), preferred_elem...  14.9 us
  transfers between devices with their start and end apart: 1, of which 1 were waited for; matrix products, arithmetic and copies ran while one was open for 0% of the time, Pallas kernels for 0%

commit v1 on v0

v1 whole, which is shorter than its diff:
```python
import functools

import jax
import jax.numpy as jnp
import numpy as np
from jax import lax
from jax.experimental import pallas as pl
from jax.experimental.pallas import tpu as pltpu
from jax.sharding import PartitionSpec as P

MESH = pl.DeviceIdType.MESH
CH = 64
BAND = 128
ROWS = 128
KVW = 512
TOK = 768
HALF = KVW // 2
MSG = HALF + 16
TOP = 32000.0
beta_decay = 0.9
step_rate = 0.1
soft_width = 0.05
F32 = jnp.float32
BF16 = jnp.bfloat16


def basis_t():
    k = np.arange(CH)[:, None]
    i = np.arange(CH)[None, :]
    w = np.where(k == 0, np.sqrt(1.0 / CH), np.sqrt(2.0 / CH))
    return (w * np.cos(np.pi * (2 * i + 1) * k / (2 * CH))).T.astype(np.float32)


def pack(out, slot, val):
    top = jnp.maximum(jnp.max(jnp.abs(val), axis=0, keepdims=True), 1e-30)
    code = jnp.ceil(jnp.log(top) * 32.0)
    inv = TOP * jnp.exp(code * (-1.0 / 32.0))
    out[slot, 0:HALF, :] = jnp.round(val * inv).astype(jnp.int32).astype(jnp.int16)
    out[slot, HALF:MSG, :] = jnp.broadcast_to(code, (16, 128)).astype(jnp.int32).astype(jnp.int16)


def unpack(buf, slot):
    code = buf[slot, HALF:MSG, :].astype(jnp.int32).astype(F32)[0:1, :]
    scale = jnp.exp(code * (1.0 / 32.0)) * (1.0 / TOP)
    return buf[slot, 0:HALF, :].astype(jnp.int32).astype(F32) * scale


def split(x):
    hi = x.astype(BF16)
    lo = (x - hi.astype(F32)).astype(BF16)
    return hi, lo


def kernel(acts, cot, mom, par, band, bt, o_mom, o_par,
           abuf, craw, ct, part, sa, ra, sb, rb, sa2, ra2, sb2, rb2, sz, rz,
           acc, w_hi, w_lo, ksel, idx, btv, momv, parv, mixed, outv, vsum,
           vrecv,
           loc, dd_s, dd_r, co_s, co_r, misc,
           sem_sa, sem_ra, sem_sb, sem_rb, sem_sa2, sem_ra2, sem_sb2, sem_rb2,
           sem_sz, sem_rz, sem_sv, sem_rv):
    f = lax.axis_index("fsdp")
    rep = lax.axis_index("rep")
    x, zh = lax.div(f, 16), lax.rem(lax.div(f, 8), 2)
    y, c = lax.rem(lax.div(f, 2), 4), lax.rem(f, 2)

    def fid(xx, zz, yy, cc):
        return ((xx * 2 + zz) * 4 + yy) * 2 + cc

    def px(d):
        return fid(lax.rem(x + d, 4), zh, y, c)

    def py(d):
        return fid(x, zh, lax.rem(y + d, 4), c)

    pz = fid(x, 1 - zh, y, c)
    pc = fid(x, zh, y, 1 - c)

    def remote(src, dst, s, r, dev):
        return pltpu.make_async_remote_copy(src, dst, s, r, device_id={"fsdp": dev}, device_id_type=MESH)

    def column(p, h, core):
        w, s, i = lax.div(p, 8), lax.rem(lax.div(p, 4), 2), lax.rem(p, 4)
        dx = lax.rem(6 - i, 4)
        dy = 2 - 2 * h + s * (4 * h - 1)
        zd = lax.rem(zh + 1 - w + 2, 2)
        return pl.multiple_of(fid(lax.rem(x + dx, 4), zd, lax.rem(y + dy, 4), core) * ROWS, ROWS)

    def own_copy(p, h):
        return pltpu.make_async_copy(acts.at[:, pl.ds(column(p, h, c), ROWS)],
                                     abuf.at[p, pl.ds(0, TOK), pl.ds(h * ROWS, ROWS)], loc.at[2 * p + h])

    def core_copy(p, h):
        return remote(acts.at[:, pl.ds(column(p, h, 1 - c), ROWS)],
                      abuf.at[p, pl.ds(TOK, TOK), pl.ds(h * ROWS, ROWS)], dd_s.at[2 * p + h], dd_r.at[2 * p + h], pc)

    cot_in = pltpu.make_async_copy(cot, craw.at[pl.ds(0, TOK)], misc.at[0])
    cot_in.start()
    small = [pltpu.make_async_copy(band, idx, misc.at[1]), pltpu.make_async_copy(bt, btv, misc.at[2]),
             pltpu.make_async_copy(mom.at[0], momv, misc.at[3]), pltpu.make_async_copy(par, parv, misc.at[4])]

    barrier = pltpu.get_barrier_semaphore()
    for dev in (pc, px(1), px(2), px(3), py(1), py(2), py(3), pz):
        pl.semaphore_signal(barrier, inc=1, device_id={"fsdp": dev}, device_id_type=MESH)
    for d in (1, 2, 3):
        pl.semaphore_signal(barrier, inc=1, device_id={"rep": lax.rem(rep + d, 4)}, device_id_type=MESH)
    for cp in small:
        cp.start()

    @pl.loop(0, 16)
    def _(p):
        own_copy(p, 0).start()
        own_copy(p, 1).start()

    pl.semaphore_wait(barrier, 11)
    cot_over = remote(cot, craw.at[pl.ds(TOK, TOK)], co_s, co_r, pc)
    cot_over.start()

    @pl.loop(0, 16)
    def _(p):
        core_copy(p, 0).start()
        core_copy(p, 1).start()

    cot_in.wait()
    ct[:, 0:TOK] = craw[0:TOK, :].T
    small[0].wait()
    small[1].wait()

    b_hi, b_lo = split(btv[...])
    b2 = jnp.concatenate([b_hi, b_lo], axis=0)
    rowid = lax.broadcasted_iota(jnp.int32, (CH, BAND), 0)

    @pl.loop(0, 8)
    def _(g):
        b, jp = lax.div(g, 4), lax.rem(g, 4)
        w_hi[g] = jnp.zeros((128, 256), BF16)
        w_lo[g] = jnp.zeros((128, 256), BF16)
        for t in range(2):
            at = idx[b, pl.ds(2 * jp + t, 1), :]
            k1 = jnp.where(rowid == jnp.right_shift(at, 6), 1.0, 0.0).astype(BF16)
            l1 = jnp.where(rowid == jnp.bitwise_and(at, 63), 1.0, 0.0).astype(BF16)
            sel = jnp.dot(b2, jnp.concatenate([k1, l1], axis=1), preferred_element_type=F32)
            ksel[g, :, 128 * t:128 * t + 128] = sel[0:64, 0:128] + sel[64:128, 0:128]
            w_hi[g, 64 * t:64 * t + 64, 128 * t:128 * t + 128] = sel[0:64, 128:256].astype(BF16)
            w_lo[g, 64 * t:64 * t + 64, 128 * t:128 * t + 128] = sel[64:128, 128:256].astype(BF16)

    cot_over.wait_recv()
    ct[:, TOK:2 * TOK] = craw[TOK:2 * TOK, :].T

    def copy_a(slot, d):
        return remote(sa.at[slot], ra.at[slot], sem_sa.at[slot], sem_ra.at[slot], px(d))

    def copy_b(slot, d):
        return remote(sb.at[slot], rb.at[slot], sem_sb.at[slot], sem_rb.at[slot], py(d))

    def half(which, slot):
        p, h = lax.div(slot, 2), lax.rem(slot, 2)
        return part[p, pl.ds(which * HALF, HALF), pl.ds(pl.multiple_of(h * ROWS, ROWS), ROWS)]

    def produce(p):
        s, i = lax.rem(lax.div(p, 4), 2), lax.rem(p, 4)
        for h in range(2):
            own_copy(p, h).wait()
            core_copy(p, h).wait_recv()
        part[p] = jnp.dot(ct[...], abuf[p], preferred_element_type=F32)
        for h in range(2):
            slot = 2 * p + h
            if h == 0:
                go_a, da = lax.rem(i, 3) == 0, 1 + 2 * lax.div(i, 3)
                go_b, db = s * (1 - lax.rem(i, 2)) == 0, 1 + 2 * lax.rem(i, 2) * (1 - s)
            else:
                go_a, da = i < 2, 3 - 2 * i
                go_b, db = s * (1 - lax.rem(i, 2)) == 1, 3

            @pl.when(go_a)
            def _():
                pack(sa, slot, part[p, 0:HALF, h * ROWS:(h + 1) * ROWS])
                copy_a(slot, da).start()

            @pl.when(go_b)
            def _():
                pack(sb, slot, part[p, HALF:KVW, h * ROWS:(h + 1) * ROWS])
                copy_b(slot, db).start()

    def relay_a(w, s):
        @pl.loop(0, 2)
        def _(h):
            got = 16 * w + 8 * s + h
            slot = got + 2 + 4 * h
            copy_a(got, 1).wait_recv()
            pack(sa, slot, unpack(ra, got) + half(0, slot))
            copy_a(slot, 1 + 2 * h).start()

    def relay_b(w):
        @pl.loop(0, 4)
        def _(i):
            odd = lax.rem(i, 2)
            got = 16 * w + 2 * i
            slot = got + 8 + odd
            copy_b(got, 1).wait_recv()
            pack(sb, slot, unpack(rb, got) + half(1, slot))
            copy_b(slot, 1 + 2 * odd).start()

    def second_a(w, q):
        return remote(sa2.at[4 * w + q], ra2.at[4 * w + q], sem_sa2.at[4 * w + q], sem_ra2.at[4 * w + q],
                      py(lax.rem(2 + 2 * lax.rem(q, 2) + lax.div(q, 2) * (3 + 4 * lax.rem(q, 2)), 4)))

    def second_b(w, i):
        return remote(sb2.at[4 * w + i], rb2.at[4 * w + i], sem_sb2.at[4 * w + i], sem_rb2.at[4 * w + i],
                      px(lax.rem(6 - i, 4)))

    def first_sum(w):
        @pl.loop(0, 4)
        def _(q):
            s, h = lax.div(q, 2), lax.rem(q, 2)
            base = 16 * w + 8 * s + h
            copy_a(base + 2, 1).wait_recv()
            copy_a(base + 6, 1).wait_recv()
            total = half(0, base + 4) + unpack(ra, base + 2) + unpack(ra, base + 6)

            @pl.when(q == 1)
            def _():
                acc[2 * w] = total

            @pl.when(q != 1)
            def _():
                pack(sa2, 4 * w + q, total)
                second_a(w, q).start()

            got = 16 * w + 8 + 2 * q
            copy_b(got, 1).wait_recv()
            copy_b(got + 1, 1).wait_recv()
            total_b = half(1, 16 * w + 2 * q + 1) + unpack(rb, got) + unpack(rb, got + 1)

            @pl.when(q == 2)
            def _():
                acc[2 * w + 1] = total_b

            @pl.when(q != 2)
            def _():
                pack(sb2, 4 * w + q, total_b)
                second_b(w, q).start()

    def second_sum(w):
        for q in (0, 2, 3):
            second_a(w, q).wait_recv()
        ga = acc[2 * w] + unpack(ra2, 4 * w) + unpack(ra2, 4 * w + 2) + unpack(ra2, 4 * w + 3)
        for q in (0, 1, 3):
            second_b(w, q).wait_recv()
        gb = acc[2 * w + 1] + unpack(rb2, 4 * w) + unpack(rb2, 4 * w + 1) + unpack(rb2, 4 * w + 3)
        return ga, gb

    cross = [remote(sz.at[n], rz.at[n], sem_sz.at[n], sem_rz.at[n], pz) for n in range(2)]

    def produce_range(a, b):
        @pl.loop(a, b)
        def _(p):
            produce(p)

    produce_range(0, 6)
    relay_a(0, 0)
    produce_range(6, 8)
    relay_b(0)
    produce_range(8, 10)
    relay_a(0, 1)
    produce_range(10, 14)
    first_sum(0)
    produce_range(14, 16)
    relay_a(1, 0)
    relay_b(1)
    relay_a(1, 1)
    ga, gb = second_sum(0)
    pack(sz, 0, ga)
    cross[0].start()
    pack(sz, 1, gb)
    cross[1].start()
    first_sum(1)
    ga, gb = second_sum(1)
    small[2].wait()
    small[3].wait()
    cross[0].wait_recv()
    ga = ga + unpack(rz, 0)
    mixed[:, 0:HALF] = beta_decay * momv[:, 0:HALF] + ga.T
    cross[1].wait_recv()
    gb = gb + unpack(rz, 1)
    mixed[:, HALF:KVW] = beta_decay * momv[:, HALF:KVW] + gb.T

    def group(g):
        b, jp = g // 4, g % 4
        return slice(64 * b, 64 * b + 64), slice(128 * jp, 128 * jp + 128)

    for g in range(8):
        rows, cols = group(g)
        hi, lo = split(mixed[rows, cols])
        q = (jnp.dot(hi, w_hi[g], preferred_element_type=F32) + jnp.dot(lo, w_hi[g], preferred_element_type=F32)
             + jnp.dot(hi, w_lo[g], preferred_element_type=F32))
        vsum[g:g + 1, :] = jnp.sum(q * ksel[g], axis=0, keepdims=True)

    swap = [pltpu.make_async_remote_copy(vsum, vrecv.at[d - 1], sem_sv.at[d - 1], sem_rv.at[d - 1],
                                         device_id={"rep": lax.rem(rep + d, 4)}, device_id_type=MESH)
            for d in (1, 2, 3)]
    for cp in swap:
        cp.start()

    def nt(a, b):
        return lax.dot_general(a, b, (((1,), (1,)), ((), ())), preferred_element_type=F32)

    def decode(values, g):
        hi, lo = split(ksel[g] * values)
        return nt(hi, w_hi[g]) + nt(lo, w_hi[g]) + nt(hi, w_lo[g])

    for g in range(8):
        rows, cols = group(g)
        mixed[rows, cols] = mixed[rows, cols] - decode(vsum[g:g + 1, :], g)
    out_m = pltpu.make_async_copy(mixed, o_mom.at[0], misc.at[5])
    out_m.start()

    for cp in swap:
        cp.wait_recv()
    shared = (vsum[...] + vrecv[0] + vrecv[1] + vrecv[2]) * 0.25
    for g in range(8):
        rows, cols = group(g)
        d = decode(shared[g:g + 1, :], g)
        outv[rows, cols] = parv[rows, cols] - step_rate * (d * lax.rsqrt(d * d + soft_width * soft_width))
    out_p = pltpu.make_async_copy(outv, o_par, misc.at[6])
    out_p.start()

    @pl.loop(0, 32)
    def _(slot):
        p, h = lax.div(slot, 2), lax.rem(slot, 2)
        s, i = lax.rem(lax.div(p, 4), 2), lax.rem(p, 4)
        core_copy(p, h).wait_send()

        @pl.when(i != 2)
        def _():
            copy_a(slot, 1).wait_send()

        @pl.when(h * (1 - s) == 0)
        def _():
            copy_b(slot, 1).wait_send()

    for w in range(2):
        for q in (0, 2, 3):
            second_a(w, q).wait_send()
        for q in (0, 1, 3):
            second_b(w, q).wait_send()
    for cp in cross + swap + [cot_over]:
        cp.wait_send()
    out_m.wait()
    out_p.wait()


def per_device(acts, cotangent, momentum, params, band_index):
    any_ = pl.BlockSpec(memory_space=pl.ANY)
    dma = pltpu.SemaphoreType.DMA
    i16 = jnp.int16
    return pl.pallas_call(
        kernel,
        out_shape=(jax.ShapeDtypeStruct((1, ROWS, KVW), F32), jax.ShapeDtypeStruct((ROWS, KVW), F32)),
        in_specs=[any_] * 6,
        out_specs=(any_, any_),
        scratch_shapes=[
            pltpu.VMEM((16, 2 * TOK, 2 * ROWS), BF16),
            pltpu.VMEM((2 * TOK, KVW), BF16),
            pltpu.VMEM((KVW, 2 * TOK), BF16),
            pltpu.VMEM((16, KVW, 2 * ROWS), F32),
            pltpu.VMEM((32, MSG, 128), i16), pltpu.VMEM((32, MSG, 128), i16),
            pltpu.VMEM((32, MSG, 128), i16), pltpu.VMEM((32, MSG, 128), i16),
            pltpu.VMEM((8, MSG, 128), i16), pltpu.VMEM((8, MSG, 128), i16),
            pltpu.VMEM((8, MSG, 128), i16), pltpu.VMEM((8, MSG, 128), i16),
            pltpu.VMEM((2, MSG, 128), i16), pltpu.VMEM((2, MSG, 128), i16),
            pltpu.VMEM((4, HALF, 128), F32),
            pltpu.VMEM((8, 128, 256), BF16), pltpu.VMEM((8, 128, 256), BF16),
            pltpu.VMEM((8, 64, 256), F32),
            pltpu.VMEM((2, 8, 128), jnp.int32),
            pltpu.VMEM((CH, CH), F32),
            pltpu.VMEM((ROWS, KVW), F32), pltpu.VMEM((ROWS, KVW), F32),
            pltpu.VMEM((ROWS, KVW), F32), pltpu.VMEM((ROWS, KVW), F32),
            pltpu.VMEM((8, 256), F32), pltpu.VMEM((3, 8, 256), F32),
            dma((32,)), dma((32,)), dma((32,)), dma, dma, dma((7,)),
            dma((32,)), dma((32,)), dma((32,)), dma((32,)),
            dma((8,)), dma((8,)), dma((8,)), dma((8,)),
            dma((2,)), dma((2,)), dma((3,)), dma((3,)),
        ],
        compiler_params=pltpu.CompilerParams(collective_id=0, has_side_effects=True, vmem_limit_bytes=56 * 2**20),
        name="step",
    )(acts, cotangent, momentum, params, band_index, jnp.asarray(basis_t()))


def solution(mesh):
    return jax.shard_map(
        per_device,
        mesh=mesh,
        in_specs=(
            P(("rep", "fsdp"), None),
            P(("rep", "fsdp"), None),
            P("rep", "fsdp", None),
            P("fsdp", None),
            P("fsdp", None, None),
        ),
        out_specs=(P("rep", "fsdp", None), P("fsdp", None)),
        check_vma=False,
    )
```

time: 536 us -> 54.5 us (0.10)
  the two profiles are of different devices: /device:TPU:32 before, /device:TPU:1 now
where the time goes in v1:
time: 54.5 us; the launch traced here: 54.4 us
  Pallas kernels  50.4 us (92%)
  local copies, waits for them, and re-layouts  3.34 us (6%)
  between operations  0.64 us (1%)
    pallas_call x1, Pallas kernels, per_device(): pl.pallas_call(kernel, out_shape=(jax.ShapeDtypeStruct((1, ROWS, KVW), F3...  50.4 us
    unnamed x2, local copies, waits for them, and re-layouts  3.34 us

profile of v1, /device:TPU:1, one launch (start us, length us, event | category | flops | bytes accessed | tf_op | source)
XLA Modules:
  0.0 54.4 jit_solution(14843144432623221935)
XLA Ops:
  0.6 50.4 %step.1 = (f32[1,128,512]{2,1,0:T(8,128)}, f32[128,512]{1,0:T(8,128)}) custom-call(bf16[768,8192]{1,0:T(8,128)(2,1)} %acts.1, bf16[768,512]{1,0:T(8,128)(2,1)} %cot.1, f32[1,128,512]{2,1,0:T(8,128)} %mom.1, f32[128,512]{1,0:T(8,128)} %par.1, s32[2,8,128]{2,1,0:T(8,128)} %band.1, f32[64,64]{1,0:T(8,128)} %constant.2.clone.bt), custom_call_target="tpu_custom_call" | custom-call | tf_op jit(solution)/shard_map/step/pallas_call | solution.py:356
  51.0 1.7 %copy.10 = f32[1,128,512]{2,1,0:T(8,128)} copy(f32[1,128,512]{2,1,0:T(8,128)} %get-tuple-element.4) | data formatting | bytes 524288
  52.7 1.7 %copy.11 = f32[128,512]{1,0:T(8,128)} copy(f32[128,512]{1,0:T(8,128)} %get-tuple-element.5) | data formatting | bytes 524288

commit v2 on v0

v2 whole, which is shorter than its diff:
```python
import functools

import jax
import jax.numpy as jnp
import numpy as np
from jax import lax
from jax.experimental import pallas as pl
from jax.experimental.pallas import tpu as pltpu
from jax.sharding import PartitionSpec as P

MESH = pl.DeviceIdType.MESH
CH = 64
BAND = 128
ROWS = 128
KVW = 512
TOK = 768
HALF = KVW // 2
TOP = 32000.0
A1, B1, A2, B2, Z = 0, 32, 64, 72, 80
N_MSG = 82
N_GROUP = 38
beta_decay = 0.9
step_rate = 0.1
soft_width = 0.05
F32 = jnp.float32
BF16 = jnp.bfloat16


def basis_t():
    i = lax.broadcasted_iota(jnp.int32, (CH, CH), 0)
    k = lax.broadcasted_iota(jnp.int32, (CH, CH), 1)
    turn = jnp.bitwise_and((2 * i + 1) * k, 4 * CH - 1).astype(F32)
    return jnp.where(k == 0, (1.0 / CH) ** 0.5, (2.0 / CH) ** 0.5) * jnp.cos(turn * (np.pi / (2 * CH)))


def pack(out, scales, slot, val):
    scale = jnp.maximum(jnp.max(jnp.abs(val), axis=0, keepdims=True), 1e-30) * (1.0 / TOP)
    out[slot] = jnp.round(val * (1.0 / scale)).astype(jnp.int32).astype(jnp.int16)
    scales[slot] = scale


def unpack(buf, scales, slot):
    return buf[slot].astype(jnp.int32).astype(F32) * scales[slot]


def split(x):
    hi = x.astype(BF16)
    lo = (x - hi.astype(F32)).astype(BF16)
    return hi, lo


def kernel(acts, cot, mom, band, mixed, own, out,
           abuf, craw, ct, part, sbuf, rbuf, sscale, rscale,
           acc, w_hi, w_lo, ksel, idx, momv, vsum, vrecv,
           loc, dd_s, dd_r, co_s, co_r, misc, sem_s, sem_r, sem_ss, sem_rs, sem_sv, sem_rv):
    f = lax.axis_index("fsdp")
    rep = lax.axis_index("rep")
    x, zh = lax.div(f, 16), lax.rem(lax.div(f, 8), 2)
    y, c = lax.rem(lax.div(f, 2), 4), lax.rem(f, 2)

    def fid(xx, zz, yy, cc):
        return ((xx * 2 + zz) * 4 + yy) * 2 + cc

    def px(d):
        return fid(lax.rem(x + d, 4), zh, y, c)

    def py(d):
        return fid(x, zh, lax.rem(y + d, 4), c)

    pz = fid(x, 1 - zh, y, c)
    pc = fid(x, zh, y, 1 - c)

    def remote(src, dst, s, r, dev):
        return pltpu.make_async_remote_copy(src, dst, s, r, device_id={"fsdp": dev}, device_id_type=MESH)

    def column(p, h, core):
        w, s, i = lax.div(p, 8), lax.rem(lax.div(p, 4), 2), lax.rem(p, 4)
        dx = lax.rem(6 - i - lax.div(i, 2) * (1 - 2 * lax.rem(i, 2)), 4)
        dy = 2 - h + s * (1 - 2 * h)
        zd = lax.rem(zh + 3 - w, 2)
        return pl.multiple_of(fid(lax.rem(x + dx, 4), zd, lax.rem(y + dy, 4), core) * ROWS, ROWS)

    def own_copy(p, h, sem):
        return pltpu.make_async_copy(acts.at[:, pl.ds(column(p, h, c), ROWS)],
                                     abuf.at[p, pl.ds(0, TOK), pl.ds(h * ROWS, ROWS)], loc.at[sem])

    def core_copy(p, h):
        return remote(acts.at[:, pl.ds(column(p, h, 1 - c), ROWS)],
                      abuf.at[p, pl.ds(TOK, TOK), pl.ds(h * ROWS, ROWS)], dd_s, dd_r.at[p], pc)

    cot_in = pltpu.make_async_copy(cot, craw.at[pl.ds(0, TOK)], misc.at[0])
    band_in = pltpu.make_async_copy(band, idx, misc.at[1])
    mom_in = pltpu.make_async_copy(mom.at[0], momv, misc.at[2])
    cot_over = [remote(cot.at[:, pl.ds(HALF * n, HALF)], craw.at[pl.ds(TOK, TOK), pl.ds(HALF * n, HALF)],
                       co_s, co_r.at[n], pc) for n in range(2)]

    barrier = pltpu.get_barrier_semaphore()
    for dev in (pc, px(1), px(2), px(3), py(1), py(2), py(3), pz):
        pl.semaphore_signal(barrier, inc=1, device_id={"fsdp": dev}, device_id_type=MESH)
    for d in (1, 2, 3):
        pl.semaphore_signal(barrier, inc=1, device_id={"rep": lax.rem(rep + d, 4)}, device_id_type=MESH)
    cot_in.start()
    own_copy(0, 0, 0).start()
    own_copy(0, 1, 0).start()
    pl.semaphore_wait(barrier, 11)
    cot_over[0].start()
    core_copy(0, 0).start()
    core_copy(0, 1).start()
    cot_over[1].start()
    band_in.start()
    mom_in.start()

    for sem, (a, b) in enumerate(((1, 6), (6, 16))):
        @pl.loop(a, b)
        def _(p):
            for h in range(2):
                core_copy(p, h).start()
                own_copy(p, h, sem + 1).start()

    cot_in.wait()
    ct[:, 0:TOK] = craw[0:TOK, :].T
    band_in.wait()

    b_hi, b_lo = split(basis_t())
    b2 = jnp.concatenate([b_hi, b_lo], axis=0)
    rowid = lax.broadcasted_iota(jnp.int32, (CH, BAND), 0)

    @pl.loop(0, 8)
    def _(g):
        b, jp = lax.div(g, 4), lax.rem(g, 4)
        w_hi[g] = jnp.zeros((128, 256), BF16)
        w_lo[g] = jnp.zeros((128, 256), BF16)
        for t in range(2):
            at = idx[b, pl.ds(2 * jp + t, 1), :]
            k1 = jnp.where(rowid == jnp.right_shift(at, 6), 1.0, 0.0).astype(BF16)
            l1 = jnp.where(rowid == jnp.bitwise_and(at, 63), 1.0, 0.0).astype(BF16)
            sel = jnp.dot(b2, jnp.concatenate([k1, l1], axis=1), preferred_element_type=F32)
            ksel[g, :, 128 * t:128 * t + 128] = sel[0:64, 0:128] + sel[64:128, 0:128]
            w_hi[g, 64 * t:64 * t + 64, 128 * t:128 * t + 128] = sel[0:64, 128:256].astype(BF16)
            w_lo[g, 64 * t:64 * t + 64, 128 * t:128 * t + 128] = sel[64:128, 128:256].astype(BF16)

    def take(group, *slots):
        n = pl.ds(0, len(slots))
        remote(rbuf.at[n], rbuf.at[n], sem_s, sem_r.at[group], pz).wait_recv()
        remote(rscale.at[n], rscale.at[n], sem_ss, sem_rs.at[group], pz).wait_recv()
        return sum(unpack(rbuf, rscale, slot) for slot in slots)

    def send(slot, group, dev, val):
        pack(sbuf, sscale, slot, val)
        remote(sbuf.at[slot], rbuf.at[slot], sem_s, sem_r.at[group], dev).start()
        remote(sscale.at[slot], rscale.at[slot], sem_ss, sem_rs.at[group], dev).start()

    def send_a1(slot, d, val):
        p, h = lax.div(slot, 2), lax.rem(slot, 2)
        send(A1 + slot, 2 * lax.div(p, 4) + h + 8 * lax.div(lax.rem(p, 4) + 3, 4), px(d), val)

    def send_b1(slot, d, val):
        p, h = lax.div(slot, 2), lax.rem(slot, 2)
        w, s, i = lax.div(p, 8), lax.rem(lax.div(p, 4), 2), lax.rem(p, 4)
        send(B1 + slot, 24 + 4 * w + i - 8 * (1 - s) * (1 - h), py(d), val)

    def send_2(n, w, q, val):
        to = (py, px)[n](2 - q + 3 * lax.div(q, 2))
        send((A2, B2)[n] + 4 * w + q, 32 + 2 * n + w, to, val)

    def half(which, slot):
        p, h = lax.div(slot, 2), lax.rem(slot, 2)
        return part[p, pl.ds(which * HALF, HALF), pl.ds(pl.multiple_of(h * ROWS, ROWS), ROWS)]

    def send_a(p):
        i = lax.rem(p, 4)
        for h in range(2):
            go, d = (lax.rem(i, 2) == 0, 1 + i) if h == 0 else (i < 2, 3 - 2 * i)

            @pl.when(go)
            def _():
                send_a1(2 * p + h, d, part[p, 0:HALF, h * ROWS:(h + 1) * ROWS])

    def send_b(p):
        s, odd = lax.rem(lax.div(p, 4), 2), lax.rem(p, 2)
        for h in range(2):
            go, d = (s * odd == 0, 1 + 2 * odd + 2 * s) if h == 0 else ((1 - s) * odd == 1, 1)

            @pl.when(go)
            def _():
                send_b1(2 * p + h, d, part[p, HALF:KVW, h * ROWS:(h + 1) * ROWS])

    def loaded(a, b, sem):
        there = abuf.at[pl.ds(a, b - a), pl.ds(0, TOK)]
        pltpu.make_async_copy(there, there, loc.at[sem]).wait()

    def arrive(p):
        there = abuf.at[p, pl.ds(TOK, TOK)]
        remote(there, there, dd_s, dd_r.at[p], pc).wait_recv()

    def produce(a, b):
        @pl.loop(a, b)
        def _(p):
            arrive(p)
            part[p] = jnp.dot(ct[...], abuf[p], preferred_element_type=F32)
            send_a(p)
            send_b(p)

    def relay_a(w, s):
        @pl.loop(0, 2)
        def _(h):
            got = 16 * w + 8 * s + h
            slot = got + 2 + 2 * h
            send_a1(slot, 1 + 2 * h, take(4 * w + 2 * s + h, A1 + got) + half(0, slot))

    def relay_b(w, a, b):
        @pl.loop(a, b)
        def _(i):
            odd = lax.rem(i, 2)
            got = 16 * w + 2 * i
            slot = got + 1 + 7 * odd
            send_b1(slot, 1 + 2 * odd, take(16 + 4 * w + i, B1 + got) + half(1, slot))

    def first_sum(w, a, b):
        @pl.loop(a, b)
        def _(q):
            base = 16 * w + 8 * lax.div(q, 2) + lax.rem(q, 2)
            total = half(0, base + 6) + take(8 + 4 * w + q, A1 + base + 2, A1 + base + 4)

            @pl.when(q == 3)
            def _():
                acc[2 * w] = total

            @pl.when(q != 3)
            def _():
                send_2(0, w, q, total)

            got = 16 * w + 2 * q
            total_b = half(1, got + 9) + take(24 + 4 * w + q, B1 + got + 1, B1 + got + 8)

            @pl.when(q == 3)
            def _():
                acc[2 * w + 1] = total_b

            @pl.when(q != 3)
            def _():
                send_2(1, w, q, total_b)

    def second_sum(w, n):
        at = (A2, B2)[n] + 4 * w
        return acc[2 * w + n] + take(32 + 2 * n + w, at, at + 1, at + 2)

    loaded(0, 1, 0)
    arrive(0)
    for n in range(2):
        cot_over[n].wait_recv()
        ct[HALF * n:HALF * n + HALF, TOK:2 * TOK] = craw[TOK:2 * TOK, HALF * n:HALF * n + HALF].T
        part[0, HALF * n:HALF * n + HALF, :] = jnp.dot(ct[HALF * n:HALF * n + HALF, :], abuf[0],
                                                       preferred_element_type=F32)
        (send_a, send_b)[n](jnp.int32(0))
    loaded(1, 6, 1)
    produce(1, 6)
    relay_a(0, 0)
    relay_b(0, 0, 3)
    loaded(6, 16, 2)
    produce(6, 8)
    relay_b(0, 3, 4)
    relay_a(0, 1)
    produce(8, 14)
    first_sum(0, 0, 4)
    produce(14, 16)
    relay_a(1, 0)
    relay_b(1, 0, 2)
    relay_a(1, 1)
    relay_b(1, 2, 4)
    for n in range(2):
        send(Z + n, 36 + n, pz, second_sum(0, n))
    first_sum(1, 0, 4)
    mom_in.wait()
    for n in range(2):
        total = second_sum(1, n) + take(36 + n, Z + n)
        cols = slice(HALF * n, HALF * n + HALF)
        mixed[:, cols] = beta_decay * momv[:, cols] + total.T

    def group(g):
        b, jp = g // 4, g % 4
        return slice(64 * b, 64 * b + 64), slice(128 * jp, 128 * jp + 128)

    for g in range(8):
        rows, cols = group(g)
        hi, lo = split(mixed[rows, cols])
        q = (jnp.dot(hi, w_hi[g], preferred_element_type=F32) + jnp.dot(lo, w_hi[g], preferred_element_type=F32)
             + jnp.dot(hi, w_lo[g], preferred_element_type=F32))
        vsum[g:g + 1, :] = jnp.sum(q * ksel[g], axis=0, keepdims=True)

    swap = [pltpu.make_async_remote_copy(vsum, vrecv.at[d - 1], sem_sv, sem_rv,
                                         device_id={"rep": lax.rem(rep + d, 4)}, device_id_type=MESH)
            for d in (1, 2, 3)]
    for cp in swap:
        cp.start()
    swapped = pltpu.make_async_remote_copy(vrecv, vrecv, sem_sv, sem_rv,
                                           device_id={"rep": lax.rem(rep + 1, 4)}, device_id_type=MESH)

    def nt(a, b):
        return lax.dot_general(a, b, (((1,), (1,)), ((), ())), preferred_element_type=F32)

    def decode(values, g):
        hi, lo = split(ksel[g] * values)
        return nt(hi, w_hi[g]) + nt(lo, w_hi[g]) + nt(hi, w_lo[g])

    for g in range(8):
        rows, cols = group(g)
        own[rows, cols] = decode(vsum[g:g + 1, :], g)

    swapped.wait_recv()
    shared = (vsum[...] + vrecv[0] + vrecv[1] + vrecv[2]) * 0.25
    for g in range(8):
        rows, cols = group(g)
        out[rows, cols] = decode(shared[g:g + 1, :], g)

    n = pl.ds(0, 62)
    remote(sbuf.at[n], rbuf.at[n], sem_s, sem_r.at[0], pz).wait_send()
    remote(sscale.at[n], rscale.at[n], sem_ss, sem_rs.at[0], pz).wait_send()
    there = abuf.at[:, pl.ds(0, TOK)]
    remote(there, there, dd_s, dd_r.at[0], pc).wait_send()
    there = craw.at[pl.ds(0, TOK)]
    remote(there, there, co_s, co_r.at[0], pc).wait_send()
    swapped.wait_send()


def per_device(acts, cotangent, momentum, params, band_index):
    any_ = pl.BlockSpec(memory_space=pl.ANY)
    dma = pltpu.SemaphoreType.DMA
    mixed, own, decoded = pl.pallas_call(
        kernel,
        out_shape=[jax.ShapeDtypeStruct((ROWS, KVW), F32)] * 3,
        in_specs=[any_] * 4,
        out_specs=[pl.BlockSpec(memory_space=pltpu.VMEM)] * 3,
        scratch_shapes=[
            pltpu.VMEM((16, 2 * TOK, 2 * ROWS), BF16),
            pltpu.VMEM((2 * TOK, KVW), BF16),
            pltpu.VMEM((KVW, 2 * TOK), BF16),
            pltpu.VMEM((16, KVW, 2 * ROWS), F32),
            pltpu.VMEM((N_MSG, HALF, 128), jnp.int16), pltpu.VMEM((N_MSG, HALF, 128), jnp.int16),
            pltpu.VMEM((N_MSG, 1, 128), F32), pltpu.VMEM((N_MSG, 1, 128), F32),
            pltpu.VMEM((4, HALF, 128), F32),
            pltpu.VMEM((8, 128, 256), BF16), pltpu.VMEM((8, 128, 256), BF16),
            pltpu.VMEM((8, 64, 256), F32),
            pltpu.VMEM((2, 8, 128), jnp.int32),
            pltpu.VMEM((ROWS, KVW), F32),
            pltpu.VMEM((8, 256), F32), pltpu.VMEM((3, 8, 256), F32),
            dma((3,)), dma, dma((16,)), dma, dma((2,)), dma((3,)),
            dma, dma((N_GROUP,)), dma, dma((N_GROUP,)), dma, dma,
        ],
        compiler_params=pltpu.CompilerParams(collective_id=0, has_side_effects=True, vmem_limit_bytes=53 * 2**20),
        name="step",
    )(acts, cotangent, momentum, band_index)
    update = decoded * lax.rsqrt(decoded * decoded + soft_width * soft_width)
    return (mixed - own)[None], params - step_rate * update


def solution(mesh):
    return jax.shard_map(
        per_device,
        mesh=mesh,
        in_specs=(
            P(("rep", "fsdp"), None),
            P(("rep", "fsdp"), None),
            P("rep", "fsdp", None),
            P("fsdp", None),
            P("fsdp", None, None),
        ),
        out_specs=(P("rep", "fsdp", None), P("fsdp", None)),
        check_vma=False,
    )
```

time: 536 us -> 48.7 us (0.09)
  the two profiles are of different devices: /device:TPU:32 before, /device:TPU:2 now
where the time goes in v2:
time: 48.7 us; the launch traced here: 47.9 us
  Pallas kernels  45.1 us (93%)
  other arithmetic  1.5 us (3%)
  local copies, waits for them, and re-layouts  0.69 us (1%)
  between operations  0.65 us (1%)
    pallas_call x1, Pallas kernels, per_device(): pl.pallas_call(kernel, out_shape=[jax.ShapeDtypeStruct((ROWS, KVW), F32)]...  45.1 us

profile of v2, /device:TPU:2, one launch (start us, length us, event | category | flops | bytes accessed | tf_op | source)
XLA Modules:
  0.0 47.9 jit_solution(17672089630801909323)
XLA Ops:
  0.6 0.0 copy-start
  0.6 0.7 %copy-done = s32[2,8,128]{2,1,0:T(8,128)S(1)} copy-done((s32[2,8,128]{2,1,0:T(8,128)S(1)}, s32[2,8,128]{2,1,0:T(8,128)}, u32[]{:S(2)}) %copy-start) | copy-done | bytes 8216
  1.3 0.0 copy-start.1
  1.3 45.1 %step.1 = (f32[128,512]{1,0:T(8,128)S(1)}, f32[128,512]{1,0:T(8,128)S(1)}, f32[128,512]{1,0:T(8,128)S(1)}) custom-call(bf16[768,8192]{1,0:T(8,128)(2,1)} %acts.1, bf16[768,512]{1,0:T(8,128)(2,1)} %cot.1, f32[1,128,512]{2,1,0:T(8,128)} %mom.1, s32[2,8,128]{2,1,0:T(8,128)S(1)} %copy-done), custom_call_target="tpu_custom_call" | custom-call | tf_op jit(solution)/shard_map/step/pallas_call | solution.py:329
  46.4 0.7 %subtract_bitcast_fusion = f32[1,128,512]{2,1,0:T(8,128)} fusion(f32[128,512]{1,0:T(8,128)S(1)} %get-tuple-element.5, f32[128,512]{1,0:T(8,128)S(1)} %get-tuple-element.6), kind=kLoop, calls=%fused_computation.1 | loop fusion | flops 65536 | bytes 786432 | tf_op jit(solution)/shard_map/broadcast_in_dim | solution.py:354
  47.2 0.0 copy-done.1
  47.2 0.8 %multiply_subtract_fusion = f32[128,512]{1,0:T(8,128)} fusion(f32[128,512]{1,0:T(8,128)S(1)} %copy-done.1, f32[128,512]{1,0:T(8,128)S(1)} %get-tuple-element.7), kind=kLoop, calls=%fused_computation | loop fusion | flops 327680 | bytes 786432 | tf_op jit(solution)/shard_map/sub | solution.py:354
Async XLA Ops:
  0.6 0.7 %copy-start = (s32[2,8,128]{2,1,0:T(8,128)S(1)}, s32[2,8,128]{2,1,0:T(8,128)}, u32[]{:S(2)}) copy-start(s32[2,8,128]{2,1,0:T(8,128)} %band.1) | copy-start | bytes 24580
  1.3 45.8 %copy-start.1 = (f32[128,512]{1,0:T(8,128)S(1)}, f32[128,512]{1,0:T(8,128)}, u32[]{:S(2)}) copy-start(f32[128,512]{1,0:T(8,128)} %param.8) | copy-start | bytes 786436

commit v3 on v2

--- a/solution.py
+++ b/solution.py
@@ -52,7 +52,7 @@
 def kernel(acts, cot, mom, band, mixed, own, out,
            abuf, craw, ct, part, sbuf, rbuf, sscale, rscale,
            acc, w_hi, w_lo, ksel, idx, momv, vsum, vrecv,
-           loc, dd_s, dd_r, co_s, co_r, misc, sem_s, sem_r, sem_ss, sem_rs, sem_sv, sem_rv):
+           loc, dd_s, dd_r, co_s, co_r, misc, sem_s, sem_r, sem_ss, sem_rs, sem_sv, sem_rv, ready_z, ready_rep):
     f = lax.axis_index("fsdp")
     rep = lax.axis_index("rep")
     x, zh = lax.div(f, 16), lax.rem(lax.div(f, 8), 2)
@@ -95,20 +95,37 @@
                        co_s, co_r.at[n], pc) for n in range(2)]
 
     barrier = pltpu.get_barrier_semaphore()
-    for dev in (pc, px(1), px(2), px(3), py(1), py(2), py(3), pz):
+    for dev in (pc, px(1), px(2), px(3), py(1), py(2), py(3)):
         pl.semaphore_signal(barrier, inc=1, device_id={"fsdp": dev}, device_id_type=MESH)
+
+    @pl.when(zh == 0)
+    def _():
+        pl.semaphore_signal(barrier, inc=1, device_id={"fsdp": pz}, device_id_type=MESH)
+
     for d in (1, 2, 3):
-        pl.semaphore_signal(barrier, inc=1, device_id={"rep": lax.rem(rep + d, 4)}, device_id_type=MESH)
+        @pl.when(rep + d < 4)
+        def _():
+            pl.semaphore_signal(barrier, inc=1, device_id={"rep": lax.rem(rep + d, 4)}, device_id_type=MESH)
+
     cot_in.start()
     own_copy(0, 0, 0).start()
     own_copy(0, 1, 0).start()
-    pl.semaphore_wait(barrier, 11)
+    pl.semaphore_wait(barrier, 7 + zh + rep)
     cot_over[0].start()
     core_copy(0, 0).start()
     core_copy(0, 1).start()
     cot_over[1].start()
     band_in.start()
     mom_in.start()
+
+    @pl.when(zh == 1)
+    def _():
+        pl.semaphore_signal(ready_z, inc=1, device_id={"fsdp": pz}, device_id_type=MESH)
+
+    for d in (1, 2, 3):
+        @pl.when(rep >= d)
+        def _():
+            pl.semaphore_signal(ready_rep, inc=1, device_id={"rep": lax.rem(rep + 4 - d, 4)}, device_id_type=MESH)
 
     for sem, (a, b) in enumerate(((1, 6), (6, 16))):
         @pl.loop(a, b)
@@ -170,7 +187,7 @@
     def send_a(p):
         i = lax.rem(p, 4)
         for h in range(2):
-            go, d = (lax.rem(i, 2) == 0, 1 + i) if h == 0 else (i < 2, 3 - 2 * i)
+            go, d = (lax.rem(i, 2) == 0, 1 + i) if h == 0 else (i + 2 * lax.div(p, 12) < 2, 3 - 2 * i)
 
             @pl.when(go)
             def _():
@@ -178,8 +195,9 @@
 
     def send_b(p):
         s, odd = lax.rem(lax.div(p, 4), 2), lax.rem(p, 2)
+        last = lax.div(p, 11) - lax.div(p, 12)
         for h in range(2):
-            go, d = (s * odd == 0, 1 + 2 * odd + 2 * s) if h == 0 else ((1 - s) * odd == 1, 1)
+            go, d = (s * odd + last == 0, 1 + 2 * odd + 2 * s) if h == 0 else ((1 - s) * odd - last == 1, 1)
 
             @pl.when(go)
             def _():
@@ -201,8 +219,14 @@
             send_a(p)
             send_b(p)
 
-    def relay_a(w, s):
-        @pl.loop(0, 2)
+    def late():
+        send_a1(25, 3, part[12, 0:HALF, ROWS:2 * ROWS])
+        send_b1(22, 3, part[11, HALF:KVW, 0:ROWS])
+        send_a1(27, 1, part[13, 0:HALF, ROWS:2 * ROWS])
+        send_b1(23, 1, part[11, HALF:KVW, ROWS:2 * ROWS])
+
+    def relay_a(w, s, a=0, b=2):
+        @pl.loop(a, b)
         def _(h):
             got = 16 * w + 8 * s + h
             slot = got + 2 + 2 * h
@@ -264,12 +288,18 @@
     produce(8, 14)
     first_sum(0, 0, 4)
     produce(14, 16)
+    late()
     relay_a(1, 0)
-    relay_b(1, 0, 2)
-    relay_a(1, 1)
-    relay_b(1, 2, 4)
+    relay_b(1, 0, 3)
+    relay_a(1, 1, 0, 1)
+    @pl.when(zh == 0)
+    def _():
+        pl.semaphore_wait(ready_z, 1)
+
     for n in range(2):
         send(Z + n, 36 + n, pz, second_sum(0, n))
+    relay_a(1, 1, 1, 2)
+    relay_b(1, 3, 4)
     first_sum(1, 0, 4)
     mom_in.wait()
     for n in range(2):
@@ -287,6 +317,10 @@
         q = (jnp.dot(hi, w_hi[g], preferred_element_type=F32) + jnp.dot(lo, w_hi[g], preferred_element_type=F32)
              + jnp.dot(hi, w_lo[g], preferred_element_type=F32))
         vsum[g:g + 1, :] = jnp.sum(q * ksel[g], axis=0, keepdims=True)
+
+    @pl.when(rep < 3)
+    def _():
+        pl.semaphore_wait(ready_rep, 3 - rep)
 
     swap = [pltpu.make_async_remote_copy(vsum, vrecv.at[d - 1], sem_sv, sem_rv,
                                          device_id={"rep": lax.rem(rep + d, 4)}, device_id_type=MESH)
@@ -346,6 +380,7 @@
             pltpu.VMEM((8, 256), F32), pltpu.VMEM((3, 8, 256), F32),
             dma((3,)), dma, dma((16,)), dma, dma((2,)), dma((3,)),
             dma, dma((N_GROUP,)), dma, dma((N_GROUP,)), dma, dma,
+            pltpu.SemaphoreType.REGULAR, pltpu.SemaphoreType.REGULAR,
         ],
         compiler_params=pltpu.CompilerParams(collective_id=0, has_side_effects=True, vmem_limit_bytes=53 * 2**20),
         name="step",

time: 48.7 us -> 46.5 us (0.955)
  Pallas kernels: 45.1 us -> 42.7 us
    pallas_call x1, Pallas kernels: 45.1 us -> 42.7 us  [per_device(): pl.pallas_call(kernel, out_shape=[jax.ShapeDtypeStruct((ROWS, KVW), F32)]...]
where the time goes in v3:
time: 46.5 us; the launch traced here: 45.5 us
  Pallas kernels  42.7 us (92%)
  other arithmetic  1.5 us (3%)
  local copies, waits for them, and re-layouts  0.69 us (1%)
  between operations  0.65 us (1%)
    pallas_call x1, Pallas kernels, per_device(): pl.pallas_call(kernel, out_shape=[jax.ShapeDtypeStruct((ROWS, KVW), F32)]...  42.7 us

profile of v3, /device:TPU:2, one launch (start us, length us, event | category | flops | bytes accessed | tf_op | source)
XLA Modules:
  0.0 45.5 jit_solution(764470339506729893)
XLA Ops:
  0.6 0.0 copy-start
  0.6 0.7 %copy-done = s32[2,8,128]{2,1,0:T(8,128)S(1)} copy-done((s32[2,8,128]{2,1,0:T(8,128)S(1)}, s32[2,8,128]{2,1,0:T(8,128)}, u32[]{:S(2)}) %copy-start) | copy-done | bytes 8216
  1.3 0.0 copy-start.1
  1.3 42.7 %step.1 = (f32[128,512]{1,0:T(8,128)S(1)}, f32[128,512]{1,0:T(8,128)S(1)}, f32[128,512]{1,0:T(8,128)S(1)}) custom-call(bf16[768,8192]{1,0:T(8,128)(2,1)} %acts.1, bf16[768,512]{1,0:T(8,128)(2,1)} %cot.1, f32[1,128,512]{2,1,0:T(8,128)} %mom.1, s32[2,8,128]{2,1,0:T(8,128)S(1)} %copy-done), custom_call_target="tpu_custom_call" | custom-call | tf_op jit(solution)/shard_map/step/pallas_call | solution.py:363
  44.0 0.7 %subtract_bitcast_fusion = f32[1,128,512]{2,1,0:T(8,128)} fusion(f32[128,512]{1,0:T(8,128)S(1)} %get-tuple-element.5, f32[128,512]{1,0:T(8,128)S(1)} %get-tuple-element.6), kind=kLoop, calls=%fused_computation.1 | loop fusion | flops 65536 | bytes 786432 | tf_op jit(solution)/shard_map/broadcast_in_dim | solution.py:389
  44.8 0.0 copy-done.1
  44.8 0.8 %multiply_subtract_fusion = f32[128,512]{1,0:T(8,128)} fusion(f32[128,512]{1,0:T(8,128)S(1)} %copy-done.1, f32[128,512]{1,0:T(8,128)S(1)} %get-tuple-element.7), kind=kLoop, calls=%fused_computation | loop fusion | flops 327680 | bytes 786432 | tf_op jit(solution)/shard_map/sub | solution.py:389
Async XLA Ops:
  0.6 0.7 %copy-start = (s32[2,8,128]{2,1,0:T(8,128)S(1)}, s32[2,8,128]{2,1,0:T(8,128)}, u32[]{:S(2)}) copy-start(s32[2,8,128]{2,1,0:T(8,128)} %band.1) | copy-start | bytes 24580
  1.3 43.4 %copy-start.1 = (f32[128,512]{1,0:T(8,128)S(1)}, f32[128,512]{1,0:T(8,128)}, u32[]{:S(2)}) copy-start(f32[128,512]{1,0:T(8,128)} %param.8) | copy-start | bytes 786436

commit v4 on v3

--- a/solution.py
+++ b/solution.py
@@ -278,14 +278,16 @@
                                                        preferred_element_type=F32)
         (send_a, send_b)[n](jnp.int32(0))
     loaded(1, 6, 1)
-    produce(1, 6)
+    produce(1, 5)
     relay_a(0, 0)
-    relay_b(0, 0, 3)
+    relay_b(0, 0, 1)
     loaded(6, 16, 2)
-    produce(6, 8)
+    produce(5, 7)
+    relay_b(0, 1, 3)
+    produce(7, 9)
     relay_b(0, 3, 4)
     relay_a(0, 1)
-    produce(8, 14)
+    produce(9, 14)
     first_sum(0, 0, 4)
     produce(14, 16)
     late()
@@ -301,22 +303,21 @@
     relay_a(1, 1, 1, 2)
     relay_b(1, 3, 4)
     first_sum(1, 0, 4)
+    def group(g):
+        b, jp = g // 4, g % 4
+        return slice(64 * b, 64 * b + 64), slice(128 * jp, 128 * jp + 128)
+
     mom_in.wait()
     for n in range(2):
         total = second_sum(1, n) + take(36 + n, Z + n)
         cols = slice(HALF * n, HALF * n + HALF)
         mixed[:, cols] = beta_decay * momv[:, cols] + total.T
-
-    def group(g):
-        b, jp = g // 4, g % 4
-        return slice(64 * b, 64 * b + 64), slice(128 * jp, 128 * jp + 128)
-
-    for g in range(8):
-        rows, cols = group(g)
-        hi, lo = split(mixed[rows, cols])
-        q = (jnp.dot(hi, w_hi[g], preferred_element_type=F32) + jnp.dot(lo, w_hi[g], preferred_element_type=F32)
-             + jnp.dot(hi, w_lo[g], preferred_element_type=F32))
-        vsum[g:g + 1, :] = jnp.sum(q * ksel[g], axis=0, keepdims=True)
+        for g in (2 * n, 2 * n + 1, 2 * n + 4, 2 * n + 5):
+            rows, lanes = group(g)
+            hi, lo = split(mixed[rows, lanes])
+            q = (jnp.dot(hi, w_hi[g], preferred_element_type=F32) + jnp.dot(lo, w_hi[g], preferred_element_type=F32)
+                 + jnp.dot(hi, w_lo[g], preferred_element_type=F32))
+            vsum[g:g + 1, :] = jnp.sum(q * ksel[g], axis=0, keepdims=True)
 
     @pl.when(rep < 3)
     def _():
@@ -384,7 +385,7 @@
         ],
         compiler_params=pltpu.CompilerParams(collective_id=0, has_side_effects=True, vmem_limit_bytes=53 * 2**20),
         name="step",
-    )(acts, cotangent, momentum, band_index)
+    )(acts, cotangent, momentum, pltpu.with_memory_space_constraint(band_index, pltpu.HBM))
     update = decoded * lax.rsqrt(decoded * decoded + soft_width * soft_width)
     return (mixed - own)[None], params - step_rate * update
 

time: 46.5 us -> 45.9 us (0.987); the launches traced: 45.5 us -> 45.8 us
  Pallas kernels: 42.7 us -> 43.7 us
  local copies, waits for them, and re-layouts: 0.69 us -> 0.01 us
    pallas_call x1, Pallas kernels: 42.7 us -> 43.7 us  [per_device(): pl.pallas_call(kernel, out_shape=[jax.ShapeDtypeStruct((ROWS, KVW), F32)]...]
    unnamed x4 -> x2, local copies, waits for them, and re-layouts: 0.69 us -> 0.01 us
where the time goes in v4:
time: 45.9 us; the launch traced here: 45.8 us
  Pallas kernels  43.7 us (95%)
  other arithmetic  1.5 us (3%)
  between operations  0.65 us (1%)
    pallas_call x1, Pallas kernels, per_device(): pl.pallas_call(kernel, out_shape=[jax.ShapeDtypeStruct((ROWS, KVW), F32)]...  43.7 us

profile of v4, /device:TPU:2, one launch (start us, length us, event | category | flops | bytes accessed | tf_op | source)
XLA Modules:
  0.0 45.8 jit_solution(7954264012535818850)
XLA Ops:
  0.6 0.0 copy-start
  0.6 43.7 %step.1 = (f32[128,512]{1,0:T(8,128)S(1)}, f32[128,512]{1,0:T(8,128)S(1)}, f32[128,512]{1,0:T(8,128)S(1)}) custom-call(bf16[768,8192]{1,0:T(8,128)(2,1)} %acts.1, bf16[768,512]{1,0:T(8,128)(2,1)} %cot.1, f32[1,128,512]{2,1,0:T(8,128)} %mom.1, s32[2,8,128]{2,1,0:T(8,128)} %band.1), custom_call_target="tpu_custom_call" | custom-call | tf_op jit(solution)/shard_map/step/pallas_call | solution.py:364
  44.3 0.7 %subtract_bitcast_fusion = f32[1,128,512]{2,1,0:T(8,128)} fusion(f32[128,512]{1,0:T(8,128)S(1)} %get-tuple-element.5, f32[128,512]{1,0:T(8,128)S(1)} %get-tuple-element.6), kind=kLoop, calls=%fused_computation.1 | loop fusion | flops 65536 | bytes 786432 | tf_op jit(solution)/shard_map/broadcast_in_dim | solution.py:390
  45.1 0.0 copy-done
  45.1 0.8 %multiply_subtract_fusion = f32[128,512]{1,0:T(8,128)} fusion(f32[128,512]{1,0:T(8,128)S(1)} %copy-done, f32[128,512]{1,0:T(8,128)S(1)} %get-tuple-element.7), kind=kLoop, calls=%fused_computation | loop fusion | flops 327680 | bytes 786432 | tf_op jit(solution)/shard_map/sub | solution.py:390
Async XLA Ops:
  0.6 44.4 %copy-start = (f32[128,512]{1,0:T(8,128)S(1)}, f32[128,512]{1,0:T(8,128)}, u32[]{:S(2)}) copy-start(f32[128,512]{1,0:T(8,128)} %param.8) | copy-start | bytes 786436

commit v5 on v4

--- a/solution.py
+++ b/solution.py
@@ -52,7 +52,7 @@
 def kernel(acts, cot, mom, band, mixed, own, out,
            abuf, craw, ct, part, sbuf, rbuf, sscale, rscale,
            acc, w_hi, w_lo, ksel, idx, momv, vsum, vrecv,
-           loc, dd_s, dd_r, co_s, co_r, misc, sem_s, sem_r, sem_ss, sem_rs, sem_sv, sem_rv, ready_z, ready_rep):
+           loc, dd_s, dd_r, co_s, co_r, misc, sem_s, sem_r, sem_ss, sem_rs, sem_sv, sem_rv, ready_x, ready_y, ready_z, ready_rep):
     f = lax.axis_index("fsdp")
     rep = lax.axis_index("rep")
     x, zh = lax.div(f, 16), lax.rem(lax.div(f, 8), 2)
@@ -95,8 +95,16 @@
                        co_s, co_r.at[n], pc) for n in range(2)]
 
     barrier = pltpu.get_barrier_semaphore()
-    for dev in (pc, px(1), px(2), px(3), py(1), py(2), py(3)):
+    for dev in (pc, px(1), px(3), py(1), py(3)):
         pl.semaphore_signal(barrier, inc=1, device_id={"fsdp": dev}, device_id_type=MESH)
+
+    @pl.when(x < 2)
+    def _():
+        pl.semaphore_signal(barrier, inc=1, device_id={"fsdp": px(2)}, device_id_type=MESH)
+
+    @pl.when(y < 2)
+    def _():
+        pl.semaphore_signal(barrier, inc=1, device_id={"fsdp": py(2)}, device_id_type=MESH)
 
     @pl.when(zh == 0)
     def _():
@@ -110,13 +118,21 @@
     cot_in.start()
     own_copy(0, 0, 0).start()
     own_copy(0, 1, 0).start()
-    pl.semaphore_wait(barrier, 7 + zh + rep)
+    pl.semaphore_wait(barrier, 5 + lax.div(x, 2) + lax.div(y, 2) + zh + rep)
     cot_over[0].start()
     core_copy(0, 0).start()
     core_copy(0, 1).start()
     cot_over[1].start()
     band_in.start()
     mom_in.start()
+
+    @pl.when(x >= 2)
+    def _():
+        pl.semaphore_signal(ready_x, inc=1, device_id={"fsdp": px(2)}, device_id_type=MESH)
+
+    @pl.when(y >= 2)
+    def _():
+        pl.semaphore_signal(ready_y, inc=1, device_id={"fsdp": py(2)}, device_id_type=MESH)
 
     @pl.when(zh == 1)
     def _():
@@ -288,6 +304,15 @@
     relay_b(0, 3, 4)
     relay_a(0, 1)
     produce(9, 14)
+
+    @pl.when(x < 2)
+    def _():
+        pl.semaphore_wait(ready_x, 1)
+
+    @pl.when(y < 2)
+    def _():
+        pl.semaphore_wait(ready_y, 1)
+
     first_sum(0, 0, 4)
     produce(14, 16)
     late()
@@ -382,6 +407,7 @@
             dma((3,)), dma, dma((16,)), dma, dma((2,)), dma((3,)),
             dma, dma((N_GROUP,)), dma, dma((N_GROUP,)), dma, dma,
             pltpu.SemaphoreType.REGULAR, pltpu.SemaphoreType.REGULAR,
+            pltpu.SemaphoreType.REGULAR, pltpu.SemaphoreType.REGULAR,
         ],
         compiler_params=pltpu.CompilerParams(collective_id=0, has_side_effects=True, vmem_limit_bytes=53 * 2**20),
         name="step",

time: 45.9 us -> 45.4 us (0.989)
  Pallas kernels: 43.7 us -> 43 us
    pallas_call x1, Pallas kernels: 43.7 us -> 43 us  [per_device(): pl.pallas_call(kernel, out_shape=[jax.ShapeDtypeStruct((ROWS, KVW), F32)]...]
where the time goes in v5:
time: 45.4 us; the launch traced here: 45.2 us
  Pallas kernels  43 us (95%)
  other arithmetic  1.5 us (3%)
  between operations  0.65 us (1%)
    pallas_call x1, Pallas kernels, per_device(): pl.pallas_call(kernel, out_shape=[jax.ShapeDtypeStruct((ROWS, KVW), F32)]...  43 us

profile of v5, /device:TPU:2, one launch (start us, length us, event | category | flops | bytes accessed | tf_op | source)
XLA Modules:
  0.0 45.2 jit_solution(532618712423598267)
XLA Ops:
  0.6 0.0 copy-start
  0.6 43.0 %step.1 = (f32[128,512]{1,0:T(8,128)S(1)}, f32[128,512]{1,0:T(8,128)S(1)}, f32[128,512]{1,0:T(8,128)S(1)}) custom-call(bf16[768,8192]{1,0:T(8,128)(2,1)} %acts.1, bf16[768,512]{1,0:T(8,128)(2,1)} %cot.1, f32[1,128,512]{2,1,0:T(8,128)} %mom.1, s32[2,8,128]{2,1,0:T(8,128)} %band.1), custom_call_target="tpu_custom_call" | custom-call | tf_op jit(solution)/shard_map/step/pallas_call | solution.py:389
  43.7 0.7 %subtract_bitcast_fusion = f32[1,128,512]{2,1,0:T(8,128)} fusion(f32[128,512]{1,0:T(8,128)S(1)} %get-tuple-element.5, f32[128,512]{1,0:T(8,128)S(1)} %get-tuple-element.6), kind=kLoop, calls=%fused_computation.1 | loop fusion | flops 65536 | bytes 786432 | tf_op jit(solution)/shard_map/broadcast_in_dim | solution.py:416
  44.4 0.0 copy-done
  44.4 0.8 %multiply_subtract_fusion = f32[128,512]{1,0:T(8,128)} fusion(f32[128,512]{1,0:T(8,128)S(1)} %copy-done, f32[128,512]{1,0:T(8,128)S(1)} %get-tuple-element.7), kind=kLoop, calls=%fused_computation | loop fusion | flops 327680 | bytes 786432 | tf_op jit(solution)/shard_map/sub | solution.py:416
Async XLA Ops:
  0.6 43.8 %copy-start = (f32[128,512]{1,0:T(8,128)S(1)}, f32[128,512]{1,0:T(8,128)}, u32[]{:S(2)}) copy-start(f32[128,512]{1,0:T(8,128)} %param.8) | copy-start | bytes 786436
